TPU v7x, 32 devices: a whole 2x2x4 slice. The times are simulated.
32 devices in a mesh: section: 2 (over core), dp: 16 (over z, y, x).
Axes of the slice: x: 2, y: 2, z: 4, core: 2. Of those that a mesh axis runs over, the one named last changes fastest.
Arguments:
- x_in: bfloat16 [2, 2048, 5120], P('section', 'dp'), may hold values from -8 to 8
- top_grad: bfloat16 [2048, 5120], P('dp'), may hold values from -6 to 6
- norm_gain: bfloat16 [2, 5120], P('section'), may hold values from 0.25 to 1.75
- proj_in: bfloat16 [2, 5120, 384], P('section', 'dp'), may hold values from -1 to 1
- proj_out: bfloat16 [2, 128, 5120], P('section', None, 'dp'), may hold values from -0.5 to 0.5
- key_cache: bfloat16 [2, 4608, 128], P('section', 'dp'), may hold values from -6 to 6
- value_cache: bfloat16 [2, 4608, 128], P('section', 'dp'), may hold values from -6 to 6
- prefix_len: int32 [16], P('dp'), may hold values from 72 to 288, as said below
- early_out: bfloat16 [2, 512, 128], P('section', 'dp'), may hold values from -0.59765625 to 0.59765625
- early_dy: bfloat16 [2, 512, 5120], P('section', 'dp'), may hold values from -6 to 6
Outputs:
- grad_x: bfloat16 [2, 2048, 5120], P('section', 'dp')
- key_cache_grad: bfloat16 [2, 4608, 128], P('section', 'dp')
- value_cache_grad: bfloat16 [2, 4608, 128], P('section', 'dp')
- wo_grad: float32 [2, 128, 5120], P('section', None, 'dp')
Inputs may be any that keep to these rules, and one draw needn't show every extreme that they name: `prefix_len`: some sequence has all 288 cached positions.
All inputs are finite; a program needn't handle non-finite values.
Results may differ from a plain program's by a relative error of at most 0.02.
Values may be sent and summed in bfloat16 or wider, within the bound.
A program may use at most 64 MiB of HBM per device.

v0:
```python
import jax
import jax.numpy as jnp
from jax import lax
from jax.sharding import PartitionSpec as P

eps = 1e-06


def passed_along(block, axis, distance):
    devices = range(lax.axis_size(axis))
    route = [(i - distance, i) for i in devices if i - distance in devices]
    return lax.ppermute(block, axis, route)


def body(
    x_in,
    top_grad,
    norm_gain,
    proj_in,
    proj_out,
    key_cache,
    value_cache,
    prefix_len,
    early_out,
    early_dy,
):
    layers = lax.axis_size("section")
    section_pos = lax.axis_index("section")
    top_section = layers - 1
    in_full, out_full = (
        lax.all_gather(proj_in, "dp", axis=1, tiled=True),
        lax.all_gather(proj_out, "dp", axis=2, tiled=True),
    )
    in_full = in_full[0]
    out_full = out_full[0]
    head_size = out_full.shape[0]
    x_rows = x_in[0]
    group_rows = x_rows.shape[0]
    width = x_rows.shape[1]
    cache_keys = key_cache[0]
    cache_rows = cache_keys.shape[0]
    key_count = cache_rows + group_rows
    score_scale = head_size ** (-0.5)
    gain_row = norm_gain[0].astype(jnp.float32)
    widened = x_rows.astype(jnp.float32)
    inv_rms = lax.rsqrt(jnp.mean(widened * widened, axis=1, keepdims=True) + eps)
    normed = (widened * inv_rms * gain_row).astype(jnp.bfloat16)
    projected = jnp.dot(normed, in_full, preferred_element_type=jnp.float32).astype(jnp.bfloat16)
    queries = projected[:, :head_size]
    all_keys = jnp.concatenate([cache_keys, projected[:, head_size : 2 * head_size]], axis=0)
    all_values = jnp.concatenate([value_cache[0], projected[:, 2 * head_size :]], axis=0)
    column = lax.broadcasted_iota(jnp.int32, (group_rows, key_count), 1)
    position = lax.broadcasted_iota(jnp.int32, (group_rows, key_count), 0)
    visible = jnp.where(
        column < cache_rows, column < prefix_len[0], column - cache_rows <= position
    )
    scores = (
        jnp.einsum("qh,kh->qk", queries, all_keys, preferred_element_type=jnp.float32) * score_scale
    )
    highest = jnp.max(jnp.where(visible, scores, -jnp.inf), axis=1, keepdims=True)
    weights = jnp.where(visible, jnp.exp(scores - highest), 0.0)
    prob_full = weights / jnp.sum(weights, axis=1, keepdims=True)
    prob_low = prob_full.astype(jnp.bfloat16)
    attended = jnp.dot(prob_low, all_values, preferred_element_type=jnp.float32).astype(
        jnp.bfloat16
    )
    part_count = 1
    part_rows = group_rows // part_count
    turn_count = layers + part_count - 1
    first_spare = jnp.where(section_pos == top_section, part_count, 0)

    def backward(part_index, grad_in, carried):
        outgoing, grad_all, key_grad, value_grad, wo_grad = carried
        part_start = part_index * part_rows
        grad_out = jnp.einsum(
            "rd,hd->rh", grad_in, out_full, preferred_element_type=jnp.float32
        ).astype(jnp.bfloat16)
        grad_prob = jnp.einsum(
            "rh,kh->rk", grad_out, all_values, preferred_element_type=jnp.float32
        )
        row_delta = jnp.sum(prob_full * grad_prob, axis=1, keepdims=True)
        grad_score = (prob_full * (grad_prob - row_delta) * score_scale).astype(jnp.bfloat16)
        grad_query = jnp.dot(grad_score, all_keys, preferred_element_type=jnp.float32)
        key_grad = key_grad + jnp.einsum(
            "rk,rh->kh", grad_score, queries, preferred_element_type=jnp.float32
        )
        value_grad = value_grad + jnp.einsum(
            "rk,rh->kh", prob_low, grad_out, preferred_element_type=jnp.float32
        )
        own_keys = lax.dynamic_slice_in_dim(key_grad, cache_rows + part_start, part_rows, 0)
        own_values = lax.dynamic_slice_in_dim(value_grad, cache_rows + part_start, part_rows, 0)
        grad_proj = jnp.concatenate([grad_query, own_keys, own_values], axis=1).astype(jnp.bfloat16)
        grad_norm = jnp.einsum("rc,dc->rd", grad_proj, in_full, preferred_element_type=jnp.float32)
        scaled = grad_norm * gain_row
        branch = inv_rms * scaled - widened * inv_rms * inv_rms * inv_rms * jnp.mean(
            widened * scaled, axis=1, keepdims=True
        )
        grad_part = (grad_in.astype(jnp.float32) + branch).astype(jnp.bfloat16)
        grad_all = grad_part
        wo_grad = wo_grad + jnp.einsum(
            "rh,rd->hd", attended, grad_in, preferred_element_type=jnp.float32
        )
        return (grad_part, grad_all, key_grad, value_grad, wo_grad)

    def advance(turn_index, carried):
        part_index = top_section - section_pos + part_count - 1 - turn_index
        active = jnp.logical_and(part_index >= 0, part_index < part_count)
        part_index = jnp.clip(part_index, 0, part_count - 1)
        grad_in = jnp.where(section_pos == top_section, top_grad, carried[0])

        def waiting(current):
            silent = (jnp.zeros_like(current[0]),) + current[1:]
            result = lax.cond(
                turn_index == first_spare,
                lambda held: held[:4]
                + (
                    held[4]
                    + jnp.einsum(
                        "eh,ed->hd", early_out[0], early_dy[0], preferred_element_type=jnp.float32
                    ),
                ),
                lambda held: held,
                silent,
            )
            return result

        return lax.cond(
            active, lambda current: backward(part_index, grad_in, current), waiting, carried
        )

    carried = (
        jnp.zeros((part_rows, width), jnp.bfloat16),
        jnp.zeros_like(x_rows),
        jnp.zeros((key_count, head_size), jnp.float32),
        jnp.zeros((key_count, head_size), jnp.float32),
        jnp.zeros((head_size, width), jnp.float32),
    )

    def one_turn(turn_index, current):
        current = advance(turn_index, current)
        passed = passed_along(current[0], "section", -1)
        return (passed,) + current[1:]

    carried = lax.fori_loop(0, turn_count - 1, one_turn, carried)
    carried = advance(turn_count - 1, carried)
    wo_grad = carried[4]
    wo_shard = lax.psum_scatter(wo_grad, "dp", scatter_dimension=1, tiled=True)
    key_out = carried[2][:cache_rows].astype(jnp.bfloat16)
    value_out = carried[3][:cache_rows].astype(jnp.bfloat16)
    return (carried[1][None], key_out[None], value_out[None], wo_shard[None])


def solution(mesh):
    in_specs = (
        P("section", "dp", None),
        P("dp", None),
        P("section", None),
        P("section", "dp", None),
        P("section", None, "dp"),
        P("section", "dp", None),
        P("section", "dp", None),
        P("dp"),
        P("section", "dp", None),
        P("section", "dp", None),
    )
    out_specs = (
        P("section", "dp", None),
        P("section", "dp", None),
        P("section", "dp", None),
        P("section", None, "dp"),
    )
    return jax.shard_map(body, mesh=mesh, in_specs=in_specs, out_specs=out_specs, check_vma=False)
```

profile of v0, /device:TPU:0, one launch (start us, length us, event | category | flops | bytes accessed | tf_op | source)
XLA Modules:
  0.0 268.9 jit_solution(12269106302307748994)
XLA Ops:
  7.2 0.0 all-gather.5.cloned.1.call-start
  7.2 0.7 all-gather.5.cloned.1.call-update
  7.9 0.0 all-gather.3.cloned.1.call-start
  7.9 0.7 all-gather.3.cloned.1.call-update
  8.6 0.0 reduce-scatter.2.cloned.1.call-start
  8.7 0.8 mul.154
  9.5 1.7 multiply_reduce_fusion.4
  11.8 1.7 broadcast_in_dim.33
  13.5 1.2 broadcast.87
  14.7 1.6 convert_bitcast_fusion
  16.3 71.2 %all-gather.5.cloned.1.call-done = bf16[1,5120,384]{2,1,0:T(8,128)(2,1)} async-done(((bf16[1,320,384]{2,1,0:T(8,128)(2,1)}), bf16[1,5120,384]{2,1,0:T(8,128)(2,1)}) %all-gather.5.cloned.1.call-update) | async-done | bytes 3932176 | tf_op jit(solution)/shard_map/all_gather | solution.py:31
  87.5 0.0 copy-start.20
  87.5 3.4 %fusion.27 = bf16[128,384]{1,0:T(8,128)(2,1)S(1)} fusion(bf16[1,128,5120]{2,1,0:T(8,128)(2,1)} %param.18, f32[5120]{0:T(1024)S(1)} %bitcast.88, f32[128]{0:T(128)S(1)} %get-tuple-element.407, bf16[1,5120,384]{2,1,0:T(8,128)(2,1)} %all-gather.5.cloned.1.call-done), kind=kOutput, calls=%fused_computation.58 | convolution fusion | flops 505987072 | bytes 5362176 | tf_op jit(solution)/shard_map/dot_general | solution.py:48
  90.9 0.0 copy-start.22
  91.0 0.0 copy-done.20
  91.0 0.0 copy-done.21
  91.0 0.7 pad_maximum_fusion
  91.7 0.3 select_reduce_fusion
  91.9 0.3 fusion.32
  92.2 0.9 fusion.38
  93.1 0.6 copy-done.14
  93.8 0.8 convolution_convert_fusion.4
  94.6 51.1 %all-gather.3.cloned.1.call-done = bf16[1,128,5120]{1,2,0:T(8,128)(2,1)} async-done(((bf16[1,128,320]{1,2,0:T(8,128)(2,1)}), bf16[1,128,5120]{1,2,0:T(8,128)(2,1)}) %all-gather.3.cloned.1.call-update) | async-done | bytes 1310736 | tf_op jit(solution)/shard_map/all_gather | solution.py:32
  145.7 0.2 select_n.40
  145.8 0.0 copy-done.22
  145.9 12.2 %conditional.4 = (bf16[128,5120]{1,0:T(8,128)(2,1)}, bf16[128,5120]{1,0:T(8,128)(2,1)}, f32[416,128]{1,0:T(8,128)S(1)}, f32[416,128]{1,0:T(8,128)}, f32[128,5120]{0,1:T(8,128)}) conditional(s32[]{:T(128)} %convert_element_type.69, (s32[]{:T(128)}, f32[128,5120]{0,1:T(8,128)}, bf16[1,32,128]{2,1,0:T(8,128)(2,1)S(1)}, bf16[1,32,5120]{2,1,0:T(8,128)(2,1)}, ...), branch_computations={%region_3.6_spmd, %region_6.9_spmd} | conditional | flops 903315328 | bytes 64692088 | solution.py:127
  145.9 3.2 %copy.23 = f32[128,5120]{1,0:T(8,128)} copy(f32[128,5120]{0,1:T(8,128)} %get-tuple-element.341) | data formatting | bytes 5242880 | tf_op jit(solution)/shard_map
  149.1 7.1 %conditional = (f32[128,5120]{0,1:T(8,128)}) conditional(s32[]{:T(128)} %convert_element_type.48, f32[128,5120]{1,0:T(8,128)} %copy.23, (bf16[1,32,128]{2,1,0:T(8,128)(2,1)S(1)}, bf16[1,32,5120]{2,1,0:T(8,128)(2,1)}, f32[128,5120]{1,0:T(8,128)}) %tuple.26), branch_computations={%region_4.4_spmd, %region_5.5_spmd} | conditional | flops 42598400 | bytes 10821640 | solution.py:113
  149.1 3.8 %convolution_add_fusion = f32[128,5120]{1,0:T(8,128)} fusion(f32[128,5120]{1,0:T(8,128)} %get-tuple-element.198, bf16[1,32,5120]{2,1,0:T(8,128)(2,1)} %get-tuple-element.200, bf16[1,32,128]{2,1,0:T(8,128)(2,1)S(1)} %get-tuple-element.199), kind=kOutput, calls=%fused_computation | convolution fusion | flops 42598400 | bytes 5578752 | tf_op jit(solution)/shard_map/while/body/eval_jaxpr/cond/branch_0_fun/cond/branch_1_fun/eh,ed->hd/dot_general | solution.py:118
  153.0 3.2 %copy.34 = f32[128,5120]{0,1:T(8,128)} copy(f32[128,5120]{1,0:T(8,128)} %convolution_add_fusion) | data formatting | bytes 5242880 | tf_op jit(solution)/shard_map
  156.2 0.7 copy.44
  156.9 1.2 broadcast.76
  158.1 1.3 collective-permute-start
  159.4 6.5 %collective-permute-done = bf16[128,5120]{1,0:T(8,128)(2,1)} collective-permute-done((bf16[128,5120]{1,0:T(8,128)(2,1)}, bf16[128,5120]{1,0:T(8,128)(2,1)}, u32[]{:S(2)}, u32[]{:S(2)}) %collective-permute-start) | collective-permute-done | bytes 1310752 | tf_op jit(solution)/shard_map/while/body/eval_jaxpr/ppermute | solution.py:12
  165.8 14.9 %conditional.5 = (bf16[128,5120]{1,0:T(8,128)(2,1)}, f32[416,128]{1,0:T(8,128)S(1)}, f32[416,128]{1,0:T(8,128)}, f32[128,5120]{0,1:T(8,128)}) conditional(s32[]{:T(128)} %convert_element_type.68, (s32[]{:T(128)}, f32[128,5120]{0,1:T(8,128)}, bf16[1,32,128]{2,1,0:T(8,128)(2,1)S(1)}, bf16[1,32,5120]{2,1,0:T(8,128)(2,1)}, ...), branch_computations={%region_9.12_spmd, %region_12.15_spmd} | conditional | flops 903315328 | bytes 62070640 | solution.py:127
  165.8 2.3 select_n.32
  168.1 0.0 copy-start.4
  168.1 0.0 copy-start.16
  168.2 0.0 copy-start.17
  168.2 1.0 copy-done.4
  169.2 0.0 copy-done.9
  169.2 0.5 convolution_convert_fusion.3
  169.7 0.0 copy-done.7
  169.7 0.0 copy-done.12
  169.7 0.2 multiply_reduce_fusion.3
  170.0 0.2 convolution_add_fusion.3
  170.2 0.0 copy-done.16
  170.2 1.8 fusion.13
  172.0 0.8 dynamic-slice_convert_fusion.2
  172.8 0.0 copy-done.17
  172.8 0.2 convolution_convert_fusion.2
  173.1 0.0 copy-start.5
  173.1 3.7 %multiply_reduce_fusion.2 = (f32[128]{0:T(128)S(1)}, f32[128,5120]{1,0:T(8,128)S(1)}) fusion(f32[128,5120]{1,0:T(8,128)S(1)} %get-tuple-element.249, f32[5120]{0:T(1024)S(1)} %get-tuple-element.248, bf16[5120,384]{1,0:T(8,128)(2,1)} %get-tuple-element.247, bf16[128,128]{1,0:T(8,128)(2,1)S(1)} %get-tuple-element.402, ...), kind=kOutput, calls=%fused_computation.31 | convolution fusion | flops 505577344 | bytes 9294336 | tf_op jit(solution)/shard_map/cond/branch_1_fun/rc,dc->rd/dot_general | solution.py:93
  176.7 0.0 copy-done.5
  176.7 0.0 copy-start.1
  176.8 0.0 copy-start.19
  176.8 1.9 add_convert_fusion.1
  178.6 0.0 copy-done.1
  178.7 0.0 copy-done.19
  178.7 2.1 fusion.12
  180.8 0.0 reduce-scatter.2.cloned.1.call-update
  180.8 0.6 fusion.33
  181.4 1.6 fusion.34
  183.0 79.3 %reduce-scatter.2.cloned.1.call-done = f32[128,320]{0,1:T(8,128)} async-done(((f32[128,5120]{0,1:T(8,128)}), f32[128,320]{0,1:T(8,128)}) %reduce-scatter.2.cloned.1.call-update) | async-done | bytes 163856 | tf_op jit(solution)/shard_map/reduce_scatter | solution.py:147
  (12 shorter events, 0.1 us)
Async XLA Ops:
  7.2 80.3 %all-gather.5.cloned.1.call-start = ((), (), s32[]{:S(2)}) async-start(), calls=%async_computation.2 | async-start | bytes 4177920 | tf_op jit(solution)/shard_map/all_gather | solution.py:31
  7.9 137.8 %all-gather.3.cloned.1.call-start = ((), (), s32[]{:S(2)}) async-start(), calls=%async_computation.1 | async-start | bytes 1392640 | tf_op jit(solution)/shard_map/all_gather | solution.py:32
  8.6 253.7 %reduce-scatter.2.cloned.1.call-start = ((), (), s32[]{:S(2)}) async-start(), calls=%async_computation.3 | async-start | bytes 2785280 | tf_op jit(solution)/shard_map/reduce_scatter | solution.py:147
  87.5 3.5 %copy-start.20 = (bf16[1,288,128]{2,1,0:T(8,128)(2,1)S(1)}, bf16[1,288,128]{2,1,0:T(8,128)(2,1)}, u32[]{:S(2)}) copy-start(bf16[1,288,128]{2,1,0:T(8,128)(2,1)} %param.23) | copy-start | bytes 221188
  87.5 3.5 %copy-start.21 = (bf16[1,288,128]{2,1,0:T(8,128)(2,1)S(1)}, bf16[1,288,128]{2,1,0:T(8,128)(2,1)}, u32[]{:S(2)}) copy-start(bf16[1,288,128]{2,1,0:T(8,128)(2,1)} %param.24) | copy-start | bytes 221188
  90.9 54.9 %copy-start.22 = (bf16[1,32,128]{2,1,0:T(8,128)(2,1)S(1)}, bf16[1,32,128]{2,1,0:T(8,128)(2,1)}, u32[]{:S(2)}) copy-start(bf16[1,32,128]{2,1,0:T(8,128)(2,1)} %param.26) | copy-start | bytes 24580
  93.1 0.6 copy-start.14
  158.1 7.8 %collective-permute-start = (bf16[128,5120]{1,0:T(8,128)(2,1)}, bf16[128,5120]{1,0:T(8,128)(2,1)}, u32[]{:S(2)}, u32[]{:S(2)}) collective-permute-start(bf16[128,5120]{1,0:T(8,128)(2,1)} %get-tuple-element.269), channel_id=1, source_target_pairs={{16,0},{17,1},{18,2},{19,3},{20,4},{21,5},{22,6},{23,7},{24,8},{25... | collective-permute-start | bytes 3932168 | tf_op jit(solution)/shard_map/while/body/eval_jaxpr/ppermute | solution.py:12
  165.8 3.4 %copy-start.9 = (bf16[128,5120]{0,1:T(8,128)(2,1)S(1)}, bf16[128,5120]{0,1:T(8,128)(2,1)}, u32[]{:S(2)}) copy-start(bf16[128,5120]{0,1:T(8,128)(2,1)} %get-tuple-element.374) | copy-start | bytes 3932164 | tf_op jit(solution)/shard_map/cond
  165.8 3.9 %copy-start.7 = (f32[128,416]{0,1:T(8,128)S(1)}, f32[128,416]{0,1:T(8,128)}, u32[]{:S(2)}) copy-start(f32[128,416]{0,1:T(8,128)} %get-tuple-element.238) | copy-start | bytes 638980 | tf_op jit(solution)/shard_map/cond
  165.8 3.9 %copy-start.12 = (bf16[416,128]{1,0:T(8,128)(2,1)S(1)}, bf16[416,128]{1,0:T(8,128)(2,1)}, u32[]{:S(2)}) copy-start(bf16[416,128]{1,0:T(8,128)(2,1)} %get-tuple-element.240) | copy-start | bytes 319492 | tf_op jit(solution)/shard_map/cond
  168.1 1.1 copy-start.4
  168.1 2.0 copy-start.16
  168.2 4.7 %copy-start.17 = (bf16[416,128]{1,0:T(8,128)(2,1)S(1)}, bf16[416,128]{1,0:T(8,128)(2,1)}, u32[]{:S(2)}) copy-start(bf16[416,128]{1,0:T(8,128)(2,1)} %get-tuple-element.241) | copy-start | bytes 319492 | tf_op jit(solution)/shard_map/cond
  173.1 3.7 %copy-start.5 = (bf16[128,5120]{1,0:T(8,128)(2,1)S(1)}, bf16[128,5120]{1,0:T(8,128)(2,1)}, u32[]{:S(2)}) copy-start(bf16[128,5120]{1,0:T(8,128)(2,1)} %copy-done.4) | copy-start | bytes 3932164 | tf_op jit(solution)/shard_map/cond
  176.7 1.9 copy-start.1
  176.8 1.9 copy-start.19
Sparse Core Ops, SparseCore 0:
  10.8 76.6 all-gather.4
  90.2 55.4 all-gather.2
  180.9 81.3 reduce-scatter.1
where the time goes:
time: 269 us
  waiting for transfers between devices  209 us (78%)
  matrix products  17.1 us (6%)
  local copies, waits for them, and re-layouts  16.2 us (6%)
  between operations  14.5 us (5%)
  other arithmetic  10.1 us (4%)
    reduce_scatter x1, waiting for transfers between devices, body(): wo_shard = lax.psum_scatter(wo_grad, 'dp', scatter_dimension=1, tiled=True)  79.3 us
    all_gather x1, waiting for transfers between devices, body(): lax.all_gather(proj_in, 'dp', axis=1, tiled=True)  71.2 us
    all_gather x1, waiting for transfers between devices, body(): lax.all_gather(proj_out, 'dp', axis=2, tiled=True)  51.1 us
    another operation x6, local copies, waits for them, and re-layouts  9.72 us
    ppermute x1, waiting for transfers between devices, passed_along(): return lax.ppermute(block, axis, route)  6.46 us
  transfers between devices with their start and end apart: 4, of which 4 were waited for; matrix products, arithmetic and copies ran while one was open for 6% of the time, Pallas kernels for 0%

commit v1 on v0

v1 whole, which is shorter than its diff:
```python
import functools

import jax
import jax.numpy as jnp
from jax import lax
from jax.experimental import pallas as pl
from jax.experimental.pallas import tpu as pltpu
from jax.sharding import PartitionSpec as P

eps = 1e-06
F32 = jnp.float32
BF16 = jnp.bfloat16
MESH = pl.DeviceIdType.MESH


def other(v, k, n):
    if n & (n - 1):
        return lax.rem(v + k, n)
    bit = 1
    while bit < n:
        if k & bit:
            v = v + bit - 2 * bit * lax.rem(v // bit, 2)
        bit *= 2
    return v


def dot(a, b, ca, cb):
    return lax.dot_general(a, b, (((ca,), (cb,)), ((), ())), preferred_element_type=F32)


def kernel(
    layers,
    sizes,
    x_ref,
    top_ref,
    gain_ref,
    wsh_ref,
    kc_ref,
    vc_ref,
    plen_ref,
    eo_ref,
    edy_ref,
    gx_ref,
    kg_ref,
    vg_ref,
    wo_ref,
    w,
    normed,
    gin,
    kall,
    vall,
    qk_acc,
    v_acc,
    go_acc,
    gproj,
    atte,
    wo_out,
    wo_in,
    w_send,
    w_recv,
    g_send,
    g_recv,
    o_send,
    o_recv,
):
    na, nb, nc = sizes
    dp = na * nb * nc
    sec = lax.axis_index("section")
    me = lax.axis_index("dp")
    top = layers - 1
    tok, width = x_ref.shape
    head = kc_ref.shape[1]
    cache = kc_ref.shape[0]
    kpad = kall.shape[0]
    shard = wsh_ref.shape[1]
    chunk = nc * shard
    chunks = width // chunk
    mz = me // (nb * nc)
    my = lax.rem(me // nc, nb)
    mx = lax.rem(me, nc)
    scale = head ** (-0.5)

    barrier = pltpu.get_barrier_semaphore()

    @pl.loop(1, dp)
    def _(k):
        pl.semaphore_signal(
            barrier, inc=1, device_id=(sec, lax.rem(me + k, dp)), device_id_type=MESH
        )

    @pl.when(sec > 0)
    def _():
        pl.semaphore_signal(barrier, inc=1, device_id=(sec - 1, me), device_id_type=MESH)

    @pl.when(sec < top)
    def _():
        pl.semaphore_signal(barrier, inc=1, device_id=(sec + 1, me), device_id_type=MESH)

    own_rows = pl.ds(pl.multiple_of(me * shard, 16), shard)
    w[:, own_rows, :] = wsh_ref[...]
    pl.semaphore_wait(barrier, dp - 1 + jnp.minimum(sec, 1) + jnp.minimum(top - sec, 1))

    def sid(kz, ky, kx):
        return (other(mz, kz, na) * nb + other(my, ky, nb)) * nc + other(mx, kx, nc)

    def piece(h, s, target, n):
        rows = w.at[h, pl.ds(pl.multiple_of(s * shard, 16), shard), :]
        return pltpu.make_async_remote_copy(
            src_ref=rows,
            dst_ref=rows,
            send_sem=w_send.at[h, n],
            recv_sem=w_recv.at[h, s],
            device_id=(sec, target),
            device_id_type=MESH,
        )

    counts = [0, 0]
    sent = []

    def send(h, s, to):
        copy = piece(h, s, sid(*to), counts[h])
        counts[h] += 1
        copy.start()
        sent.append(copy)

    def arrive(h, s):
        piece(h, s, lax.rem(me + 1, dp), 0).wait_recv()

    nmid = (nb, nc)
    nlast = (nc, nb)

    def at(h, kz, mid, last):
        return (kz, mid, last) if h == 0 else (kz, last, mid)

    def send_mid(h, s):
        for m in range(1, nmid[h]):
            send(h, s, at(h, 0, m, 0))

    def send_last(h, s):
        for m in range(1, nlast[h]):
            send(h, s, at(h, 0, 0, m))

    for kz in range(1, na):
        for h in range(2):
            send(h, me, (kz, 0, 0))
    for h in range(2):
        send_mid(h, me)
    for h in range(2):
        send_last(h, me)

    gin[tok:, :] = edy_ref[...]
    atte[tok:, :] = eo_ref[...]
    kall[:cache, :] = kc_ref[...]
    vall[:cache, :] = vc_ref[...]
    if kpad > cache + tok:
        kall[cache + tok :, :] = jnp.zeros((kpad - cache - tok, head), BF16)
        vall[cache + tok :, :] = jnp.zeros((kpad - cache - tok, head), BF16)
    qk_acc[...] = jnp.zeros_like(qk_acc)
    v_acc[...] = jnp.zeros_like(v_acc)
    go_acc[...] = jnp.zeros_like(go_acc)

    @pl.when(sec == top)
    def _():
        gin[:tok, :] = top_ref[...]

    def columns(c):
        return pl.ds(pl.multiple_of(c * chunk, 128), chunk)

    def squares(c, total):
        part = x_ref[:, columns(c)].astype(F32)
        return total + jnp.sum(part * part, axis=1, keepdims=True)

    total = lax.fori_loop(0, chunks, squares, jnp.zeros((tok, 1), F32))
    inv_rms = lax.rsqrt(total / width + eps)

    @pl.loop(0, chunks)
    def _(c):
        part = x_ref[:, columns(c)].astype(F32)
        gain = gain_ref[:, columns(c)].astype(F32)
        normed[:, columns(c)] = (part * inv_rms * gain).astype(BF16)

    def add_grad_out(c):
        go_acc[...] += dot(gin[:tok, columns(c)], w[1, columns(c), head:], 1, 0)

    def use(kz):
        for ky in range(nb):
            for h in range(2):
                for kx in range(nc):
                    if (kx if h == 0 else ky) > 0:
                        arrive(h, sid(kz, ky, kx))
            c = other(mz, kz, na) * nb + other(my, ky, nb)
            part = normed[:, columns(c)]
            qk_acc[...] += dot(part, w[0, columns(c), :], 1, 0)
            v_acc[...] += dot(part, w[1, columns(c), :head], 1, 0)

            @pl.when(sec == top)
            def _():
                add_grad_out(c)

    for kz in range(na):
        if kz > 0:
            for h in range(2):
                s = sid(kz, 0, 0)
                arrive(h, s)
                send_mid(h, s)
                send_last(h, s)
        for h in range(2):
            for m in range(1, nmid[h]):
                s = sid(*at(h, kz, m, 0))
                arrive(h, s)
                send_last(h, s)
        if kz > 0:
            use(kz - 1)
    use(na - 1)

    query = qk_acc[:, :head].astype(BF16)
    kall[cache : cache + tok, :] = qk_acc[:, head:].astype(BF16)
    vall[cache : cache + tok, :] = v_acc[...].astype(BF16)
    column = lax.broadcasted_iota(jnp.int32, (tok, kpad), 1)
    position = lax.broadcasted_iota(jnp.int32, (tok, kpad), 0)
    limit = jnp.where(column < cache, plen_ref[0], position + cache + 1)
    visible = column < limit
    scores = dot(query, kall[...], 1, 1) * scale
    highest = jnp.max(jnp.where(visible, scores, -jnp.inf), axis=1, keepdims=True)
    weights = jnp.where(visible, jnp.exp(scores - highest), 0.0)
    prob = weights / jnp.sum(weights, axis=1, keepdims=True)
    prob_low = prob.astype(BF16)
    atte[:tok, :] = dot(prob_low, vall[...], 1, 0).astype(BF16)

    def relay(c):
        return pltpu.make_async_remote_copy(
            src_ref=gx_ref.at[:, columns(c)],
            dst_ref=gin.at[pl.ds(0, tok), columns(c)],
            send_sem=g_send.at[c],
            recv_sem=g_recv.at[c],
            device_id=(jnp.maximum(sec - 1, 0), me),
            device_id_type=MESH,
        )

    def relay_in(c):
        return pltpu.make_async_remote_copy(
            src_ref=gx_ref.at[:, columns(c)],
            dst_ref=gin.at[pl.ds(0, tok), columns(c)],
            send_sem=g_send.at[c],
            recv_sem=g_recv.at[c],
            device_id=(jnp.minimum(sec + 1, top), me),
            device_id_type=MESH,
        )

    def share(owner, source):
        return pltpu.make_async_remote_copy(
            src_ref=wo_out.at[pl.ds(pl.multiple_of(owner * shard, 16), shard), :],
            dst_ref=wo_in.at[source],
            send_sem=o_send.at[owner],
            recv_sem=o_recv.at[source],
            device_id=(sec, owner),
            device_id_type=MESH,
        )

    def wo_chunk(c):
        both = dot(gin[:, columns(c)], atte[...], 0, 0)
        wo_out[columns(c), :] = both.astype(BF16)
        for j in range(nc):
            owner = c * nc + j

            @pl.when(owner != me)
            def _():
                share(owner, me).start()

    @pl.when(sec < top)
    def _():
        @pl.loop(0, chunks)
        def _(c):
            relay_in(c).wait_recv()
            add_grad_out(c)

            @pl.when(sec == 0)
            def _():
                wo_chunk(c)

    grad_out = go_acc[...].astype(BF16)
    grad_prob = dot(grad_out, vall[...], 1, 1)
    row_delta = jnp.sum(prob * grad_prob, axis=1, keepdims=True)
    grad_score = (prob * (grad_prob - row_delta) * scale).astype(BF16)
    grad_query = dot(grad_score, kall[...], 1, 0)
    grad_keys = dot(grad_score, query, 0, 0)
    grad_values = dot(prob_low, grad_out, 0, 0)
    kg_ref[...] = grad_keys[:cache].astype(BF16)
    vg_ref[...] = grad_values[:cache].astype(BF16)
    gproj[:, :head] = grad_query.astype(BF16)
    gproj[:, head : 2 * head] = grad_keys[cache : cache + tok].astype(BF16)
    gproj[:, 2 * head :] = grad_values[cache : cache + tok].astype(BF16)
    g_qk = gproj[:, : 2 * head]
    g_v = gproj[:, 2 * head :]
    row_sum = jnp.sum(g_qk.astype(F32) * qk_acc[...], axis=1, keepdims=True) + jnp.sum(
        g_v.astype(F32) * v_acc[...], axis=1, keepdims=True
    )
    pull = inv_rms * inv_rms * (row_sum / width)

    @pl.loop(0, chunks)
    def _(c):
        grad_norm = dot(g_qk, w[0, columns(c), :], 1, 1) + dot(g_v, w[1, columns(c), :head], 1, 1)
        scaled = grad_norm * gain_ref[:, columns(c)].astype(F32)
        branch = inv_rms * scaled - x_ref[:, columns(c)].astype(F32) * pull
        gx_ref[:, columns(c)] = (gin[:tok, columns(c)].astype(F32) + branch).astype(BF16)

        @pl.when(sec > 0)
        def _():
            relay(c).start()

    @pl.when(jnp.logical_or(sec > 0, top == 0))
    def _():
        @pl.loop(0, chunks)
        def _(c):
            wo_chunk(c)

    for copy in sent:
        copy.wait_send()

    @pl.when(sec > 0)
    def _():
        @pl.loop(0, chunks)
        def _(c):
            relay(c).wait_send()

    @pl.loop(1, dp)
    def _(k):
        share(lax.rem(me + k, dp), me).wait_send()

    @pl.loop(1, dp)
    def _(k):
        share(lax.rem(me + 1, dp), lax.rem(me + k, dp)).wait_recv()

    def gathered(k, part):
        return part + wo_in[lax.rem(me + k, dp)].astype(F32)

    part = lax.fori_loop(1, dp, gathered, wo_out[own_rows, :].astype(F32))
    wo_ref[...] = part


def body(
    layers,
    dp,
    x_in,
    top_grad,
    norm_gain,
    proj_in,
    proj_out,
    key_cache,
    value_cache,
    prefix_len,
    early_out,
    early_dy,
):
    tok, width = x_in.shape[1:]
    shard = proj_in.shape[1]
    head = proj_out.shape[1]
    cache = key_cache.shape[1]
    erows = early_out.shape[1]
    nc = 1
    while (nc * shard) % 128:
        nc *= 2
    nb = 2 if (dp // nc) % 2 == 0 else 1
    na = dp // (nc * nb)
    kpad = -(-(cache + tok) // 128) * 128
    chunks = dp // nc
    shards = jnp.stack(
        [
            proj_in[0, :, : 2 * head],
            jnp.concatenate([proj_in[0, :, 2 * head :], proj_out[0].T], axis=1),
        ]
    )
    vmem = pl.BlockSpec(memory_space=pltpu.VMEM)
    smem = pl.BlockSpec(memory_space=pltpu.SMEM)
    outs = pl.pallas_call(
        functools.partial(kernel, layers, (na, nb, nc)),
        out_shape=(
            jax.ShapeDtypeStruct((tok, width), BF16),
            jax.ShapeDtypeStruct((cache, head), BF16),
            jax.ShapeDtypeStruct((cache, head), BF16),
            jax.ShapeDtypeStruct((shard, head), F32),
        ),
        in_specs=[vmem] * 6 + [smem] + [vmem] * 2,
        out_specs=(vmem,) * 4,
        scratch_shapes=[
            pltpu.VMEM((2, width, 2 * head), BF16),
            pltpu.VMEM((tok, width), BF16),
            pltpu.VMEM((tok + erows, width), BF16),
            pltpu.VMEM((kpad, head), BF16),
            pltpu.VMEM((kpad, head), BF16),
            pltpu.VMEM((tok, 2 * head), F32),
            pltpu.VMEM((tok, head), F32),
            pltpu.VMEM((tok, head), F32),
            pltpu.VMEM((tok, 3 * head), BF16),
            pltpu.VMEM((tok + erows, head), BF16),
            pltpu.VMEM((width, head), BF16),
            pltpu.VMEM((dp, shard, head), BF16),
            pltpu.SemaphoreType.DMA((2, dp)),
            pltpu.SemaphoreType.DMA((2, dp)),
            pltpu.SemaphoreType.DMA((chunks,)),
            pltpu.SemaphoreType.DMA((chunks,)),
            pltpu.SemaphoreType.DMA((dp,)),
            pltpu.SemaphoreType.DMA((dp,)),
        ],
        compiler_params=pltpu.CompilerParams(
            collective_id=0, has_side_effects=True, vmem_limit_bytes=48 * 1024 * 1024
        ),
        cost_estimate=pl.CostEstimate(
            flops=8 * tok * width * head * 4, bytes_accessed=8 * tok * width, transcendentals=0
        ),
        name="window_backward",
    )(
        x_in[0],
        top_grad,
        norm_gain,
        shards,
        key_cache[0],
        value_cache[0],
        prefix_len,
        early_out[0],
        early_dy[0],
    )
    grad_x, key_grad, value_grad, wo_grad = outs
    return grad_x[None], key_grad[None], value_grad[None], wo_grad.T[None]


def solution(mesh):
    in_specs = (
        P("section", "dp", None),
        P("dp", None),
        P("section", None),
        P("section", "dp", None),
        P("section", None, "dp"),
        P("section", "dp", None),
        P("section", "dp", None),
        P("dp"),
        P("section", "dp", None),
        P("section", "dp", None),
    )
    out_specs = (
        P("section", "dp", None),
        P("section", "dp", None),
        P("section", "dp", None),
        P("section", None, "dp"),
    )
    fn = functools.partial(body, mesh.shape["section"], mesh.shape["dp"])
    return jax.shard_map(fn, mesh=mesh, in_specs=in_specs, out_specs=out_specs, check_vma=False)
```

time: 269 us -> 93.5 us (0.35)
  the two profiles are of different devices: /device:TPU:0 before, /device:TPU:30 now
where the time goes in v1:
time: 93.5 us; the launch traced here: 93.3 us
  Pallas kernels  83.7 us (90%)
  local copies, waits for them, and re-layouts  7.12 us (8%)
  between operations  1.5 us (2%)
  other arithmetic  0.94 us (1%)
    pallas_call x1, Pallas kernels, body(): pl.pallas_call(functools.partial(kernel, layers, (na, nb, nc)), out_shape...  83.7 us
    unnamed x18, local copies, waits for them, and re-layouts  5.29 us

profile of v1, /device:TPU:30, one launch (start us, length us, event | category | flops | bytes accessed | tf_op | source)
XLA Modules:
  0.0 93.3 jit_solution(579704562111648609)
XLA Ops:
  0.6 0.0 copy-start.6
  0.6 0.0 copy-start.4
  0.7 0.0 copy-start.3
  0.7 0.0 copy-start.5
  0.7 0.0 copy-start
  1.4 0.9 slice_bitcast_fusion
  2.3 0.9 maximum_bitcast_fusion
  3.2 0.9 slice.6
  4.2 0.0 copy-done.6
  4.2 0.0 copy-done.4
  4.2 0.0 copy-done.3
  4.2 0.0 copy-done.5
  4.3 0.0 copy-done
  4.3 0.0 copy-start.1
  4.3 1.3 %copy-done.1 = bf16[128,5120]{1,0:T(8,128)(2,1)S(1)} copy-done((bf16[128,5120]{1,0:T(8,128)(2,1)S(1)}, bf16[128,5120]{1,0:T(8,128)(2,1)}, u32[]{:S(2)}) %copy-start.1) | copy-done | bytes 1310744
  5.6 0.0 copy-start.2
  5.6 1.0 %copy-done.2 = bf16[1,32,5120]{2,1,0:T(8,128)(2,1)S(1)} copy-done((bf16[1,32,5120]{2,1,0:T(8,128)(2,1)S(1)}, bf16[1,32,5120]{2,1,0:T(8,128)(2,1)}, u32[]{:S(2)}) %copy-start.2) | copy-done | bytes 327704
  6.6 83.7 %window_backward.1 = (bf16[128,5120]{1,0:T(8,128)(2,1)S(1)}, bf16[288,128]{1,0:T(8,128)(2,1)S(1)}, bf16[288,128]{1,0:T(8,128)(2,1)S(1)}, f32[320,128]{1,0:T(8,128)S(1)}) custom-call(bf16[128,5120]{1,0:T(8,128)(2,1)S(1)} %bitcast.22, bf16[128,5120]{1,0:T(8,128)(2,1)S(1)} %copy-done.1, bf16[1,5120]{1,0:T(2,128)(2,1)S(1)} %copy-done.5, ...), custom_call_target="tpu_custom_call" | custom-call | flops 2684354560 | bytes 5242880 | tf_op jit(solution)/shard_map/window_backward/pallas_call | solution.py:375
  90.3 1.1 %copy.19 = bf16[1,128,5120]{2,1,0:T(8,128)(2,1)} copy(bf16[1,128,5120]{2,1,0:T(8,128)(2,1)S(1)} %bitcast.18) | data formatting | bytes 2621440
  91.3 0.6 copy.20
  92.0 0.6 copy.21
  92.6 0.7 copy.22
  (1 shorter events, 0.0 us)
Async XLA Ops:
  0.6 3.6 %copy-start.6 = (bf16[1,32,128]{2,1,0:T(8,128)(2,1)S(1)}, bf16[1,32,128]{2,1,0:T(8,128)(2,1)}, u32[]{:S(2)}) copy-start(bf16[1,32,128]{2,1,0:T(8,128)(2,1)} %param.18) | copy-start | bytes 24580
  0.6 3.6 %copy-start.4 = (bf16[1,288,128]{2,1,0:T(8,128)(2,1)S(1)}, bf16[1,288,128]{2,1,0:T(8,128)(2,1)}, u32[]{:S(2)}) copy-start(bf16[1,288,128]{2,1,0:T(8,128)(2,1)} %param.16) | copy-start | bytes 221188
  0.7 3.6 %copy-start.3 = (bf16[1,288,128]{2,1,0:T(8,128)(2,1)S(1)}, bf16[1,288,128]{2,1,0:T(8,128)(2,1)}, u32[]{:S(2)}) copy-start(bf16[1,288,128]{2,1,0:T(8,128)(2,1)} %param.15) | copy-start | bytes 221188
  0.7 3.6 %copy-start.5 = (bf16[1,5120]{1,0:T(2,128)(2,1)S(1)}, bf16[1,5120]{1,0:T(2,128)(2,1)}, u32[]{:S(2)}) copy-start(bf16[1,5120]{1,0:T(2,128)(2,1)} %gain_ref.1) | copy-start | bytes 30724
  0.7 3.6 %copy-start = (bf16[1,128,5120]{2,1,0:T(8,128)(2,1)S(1)}, bf16[1,128,5120]{2,1,0:T(8,128)(2,1)}, u32[]{:S(2)}) copy-start(bf16[1,128,5120]{2,1,0:T(8,128)(2,1)} %param.10) | copy-start | bytes 3932164
  4.3 1.3 %copy-start.1 = (bf16[128,5120]{1,0:T(8,128)(2,1)S(1)}, bf16[128,5120]{1,0:T(8,128)(2,1)}, u32[]{:S(2)}) copy-start(bf16[128,5120]{1,0:T(8,128)(2,1)} %top_ref.1) | copy-start | bytes 3932164
  5.6 1.0 %copy-start.2 = (bf16[1,32,5120]{2,1,0:T(8,128)(2,1)S(1)}, bf16[1,32,5120]{2,1,0:T(8,128)(2,1)}, u32[]{:S(2)}) copy-start(bf16[1,32,5120]{2,1,0:T(8,128)(2,1)} %param.19) | copy-start | bytes 983044

commit v2 on v1

--- a/solution.py
+++ b/solution.py
@@ -31,10 +31,11 @@
 def kernel(
     layers,
     sizes,
-    x_ref,
+    x_hbm,
     top_ref,
     gain_ref,
-    wsh_ref,
+    in_ref,
+    out_ref,
     kc_ref,
     vc_ref,
     plen_ref,
@@ -45,6 +46,7 @@
     vg_ref,
     wo_ref,
     w,
+    x_ref,
     normed,
     gin,
     kall,
@@ -55,11 +57,16 @@
     gproj,
     atte,
     wo_out,
+    wo_mid,
+    wo_sum,
     wo_in,
+    load,
     w_send,
     w_recv,
     g_send,
     g_recv,
+    m_send,
+    m_recv,
     o_send,
     o_recv,
 ):
@@ -72,7 +79,7 @@
     head = kc_ref.shape[1]
     cache = kc_ref.shape[0]
     kpad = kall.shape[0]
-    shard = wsh_ref.shape[1]
+    shard = in_ref.shape[0]
     chunk = nc * shard
     chunks = width // chunk
     mz = me // (nb * nc)
@@ -97,7 +104,31 @@
         pl.semaphore_signal(barrier, inc=1, device_id=(sec + 1, me), device_id_type=MESH)
 
     own_rows = pl.ds(pl.multiple_of(me * shard, 16), shard)
-    w[:, own_rows, :] = wsh_ref[...]
+    loads = [
+        pltpu.make_async_copy(source, target, load.at[n])
+        for n, (source, target) in enumerate(
+            [
+                (in_ref.at[:, pl.ds(0, 2 * head)], w.at[0, own_rows, :]),
+                (in_ref.at[:, pl.ds(2 * head, head)], w.at[1, own_rows, pl.ds(0, head)]),
+                (out_ref, w.at[1, own_rows, pl.ds(head, head)]),
+                (x_hbm, x_ref),
+                (kc_ref, kall.at[pl.ds(0, cache), :]),
+                (vc_ref, vall.at[pl.ds(0, cache), :]),
+                (eo_ref, atte.at[pl.ds(tok, eo_ref.shape[0]), :]),
+                (edy_ref, gin.at[pl.ds(tok, eo_ref.shape[0]), :]),
+                (top_ref, gin.at[pl.ds(0, tok), :]),
+            ]
+        )
+    ]
+    for copy in loads[:-1]:
+        copy.start()
+
+    @pl.when(sec == top)
+    def _():
+        loads[-1].start()
+
+    for copy in loads[:3]:
+        copy.wait()
     pl.semaphore_wait(barrier, dp - 1 + jnp.minimum(sec, 1) + jnp.minimum(top - sec, 1))
 
     def sid(kz, ky, kx):
@@ -148,10 +179,6 @@
     for h in range(2):
         send_last(h, me)
 
-    gin[tok:, :] = edy_ref[...]
-    atte[tok:, :] = eo_ref[...]
-    kall[:cache, :] = kc_ref[...]
-    vall[:cache, :] = vc_ref[...]
     if kpad > cache + tok:
         kall[cache + tok :, :] = jnp.zeros((kpad - cache - tok, head), BF16)
         vall[cache + tok :, :] = jnp.zeros((kpad - cache - tok, head), BF16)
@@ -159,9 +186,12 @@
     v_acc[...] = jnp.zeros_like(v_acc)
     go_acc[...] = jnp.zeros_like(go_acc)
 
+    for copy in loads[3:-1]:
+        copy.wait()
+
     @pl.when(sec == top)
     def _():
-        gin[:tok, :] = top_ref[...]
+        loads[-1].wait()
 
     def columns(c):
         return pl.ds(pl.multiple_of(c * chunk, 128), chunk)
@@ -247,36 +277,68 @@
             device_id_type=MESH,
         )
 
-    def share(owner, source):
+    group = me // nc
+
+    def order(i):
+        return lax.rem(group + 1 + i, chunks)
+
+    def block(c, j):
+        return pl.ds(pl.multiple_of((c * nc + j) * shard, 16), shard)
+
+    def mid(c, j, source):
         return pltpu.make_async_remote_copy(
-            src_ref=wo_out.at[pl.ds(pl.multiple_of(owner * shard, 16), shard), :],
+            src_ref=wo_out.at[block(c, j), :],
+            dst_ref=wo_mid.at[c, source],
+            send_sem=m_send.at[c, j],
+            recv_sem=m_recv.at[c, source],
+            device_id=(sec, group * nc + j),
+            device_id_type=MESH,
+        )
+
+    def share(c, source):
+        return pltpu.make_async_remote_copy(
+            src_ref=wo_sum.at[c],
             dst_ref=wo_in.at[source],
-            send_sem=o_send.at[owner],
+            send_sem=o_send.at[c],
             recv_sem=o_recv.at[source],
-            device_id=(sec, owner),
+            device_id=(sec, c * nc + mx),
             device_id_type=MESH,
         )
 
     def wo_chunk(c):
         both = dot(gin[:, columns(c)], atte[...], 0, 0)
         wo_out[columns(c), :] = both.astype(BF16)
-        for j in range(nc):
-            owner = c * nc + j
-
-            @pl.when(owner != me)
-            def _():
-                share(owner, me).start()
-
-    @pl.when(sec < top)
-    def _():
-        @pl.loop(0, chunks)
-        def _(c):
+        for k in range(1, nc):
+            mid(c, other(mx, k, nc), mx).start()
+
+    def wo_pass(c):
+        part = wo_out[block(c, mx), :].astype(F32)
+        for k in range(1, nc):
+            j = other(mx, k, nc)
+            mid(c, j, j).wait_recv()
+            part = part + wo_mid[c, j].astype(F32)
+        wo_sum[c] = part.astype(BF16)
+
+        @pl.when(c != group)
+        def _():
+            share(c, group).start()
+
+    lag = min(2, chunks)
+
+    @pl.loop(0, chunks)
+    def _(i):
+        c = order(i)
+
+        @pl.when(sec < top)
+        def _():
             relay_in(c).wait_recv()
             add_grad_out(c)
 
-            @pl.when(sec == 0)
-            def _():
-                wo_chunk(c)
+        wo_chunk(c)
+
+        @pl.when(jnp.logical_and(sec < top, i >= lag))
+        def _():
+            wo_pass(order(i - lag))
 
     grad_out = go_acc[...].astype(BF16)
     grad_prob = dot(grad_out, vall[...], 1, 1)
@@ -297,8 +359,15 @@
     )
     pull = inv_rms * inv_rms * (row_sum / width)
 
+    @pl.when(sec < top)
+    def _():
+        @pl.loop(chunks - lag, chunks)
+        def _(i):
+            wo_pass(order(i))
+
     @pl.loop(0, chunks)
-    def _(c):
+    def _(i):
+        c = order(i)
         grad_norm = dot(g_qk, w[0, columns(c), :], 1, 1) + dot(g_v, w[1, columns(c), :head], 1, 1)
         scaled = grad_norm * gain_ref[:, columns(c)].astype(F32)
         branch = inv_rms * scaled - x_ref[:, columns(c)].astype(F32) * pull
@@ -308,34 +377,44 @@
         def _():
             relay(c).start()
 
-    @pl.when(jnp.logical_or(sec > 0, top == 0))
-    def _():
-        @pl.loop(0, chunks)
-        def _(c):
-            wo_chunk(c)
+        @pl.when(sec == top)
+        def _():
+            wo_pass(c)
 
     for copy in sent:
         copy.wait_send()
 
-    @pl.when(sec > 0)
-    def _():
-        @pl.loop(0, chunks)
-        def _(c):
+    @pl.loop(0, chunks)
+    def _(c):
+        @pl.when(sec > 0)
+        def _():
             relay(c).wait_send()
 
-    @pl.loop(1, dp)
-    def _(k):
-        share(lax.rem(me + k, dp), me).wait_send()
-
-    @pl.loop(1, dp)
-    def _(k):
-        share(lax.rem(me + 1, dp), lax.rem(me + k, dp)).wait_recv()
-
-    def gathered(k, part):
-        return part + wo_in[lax.rem(me + k, dp)].astype(F32)
-
-    part = lax.fori_loop(1, dp, gathered, wo_out[own_rows, :].astype(F32))
-    wo_ref[...] = part
+        for k in range(1, nc):
+            mid(c, other(mx, k, nc), mx).wait_send()
+
+        @pl.when(c != group)
+        def _():
+            share(c, group).wait_send()
+
+    def gathered(i, part):
+        source = order(i)
+        share(group, source).wait_recv()
+        return part + wo_in[source].astype(F32)
+
+    wo_ref[...] = lax.fori_loop(0, chunks - 1, gathered, wo_sum[group].astype(F32))
+
+
+def results(*refs):
+    sems = refs[-1]
+    count = len(refs) // 2
+    copies = [
+        pltpu.make_async_copy(refs[n], refs[count + n], sems.at[n]) for n in range(count)
+    ]
+    for copy in copies:
+        copy.start()
+    for copy in copies:
+        copy.wait()
 
 
 def body(
@@ -364,13 +443,8 @@
     na = dp // (nc * nb)
     kpad = -(-(cache + tok) // 128) * 128
     chunks = dp // nc
-    shards = jnp.stack(
-        [
-            proj_in[0, :, : 2 * head],
-            jnp.concatenate([proj_in[0, :, 2 * head :], proj_out[0].T], axis=1),
-        ]
-    )
     vmem = pl.BlockSpec(memory_space=pltpu.VMEM)
+    anywhere = pl.BlockSpec(memory_space=pltpu.HBM)
     smem = pl.BlockSpec(memory_space=pltpu.SMEM)
     outs = pl.pallas_call(
         functools.partial(kernel, layers, (na, nb, nc)),
@@ -380,10 +454,11 @@
             jax.ShapeDtypeStruct((cache, head), BF16),
             jax.ShapeDtypeStruct((shard, head), F32),
         ),
-        in_specs=[vmem] * 6 + [smem] + [vmem] * 2,
+        in_specs=[anywhere] * 2 + [vmem] + [anywhere] * 4 + [smem] + [anywhere] * 2,
         out_specs=(vmem,) * 4,
         scratch_shapes=[
             pltpu.VMEM((2, width, 2 * head), BF16),
+            pltpu.VMEM((tok, width), BF16),
             pltpu.VMEM((tok, width), BF16),
             pltpu.VMEM((tok + erows, width), BF16),
             pltpu.VMEM((kpad, head), BF16),
@@ -394,13 +469,18 @@
             pltpu.VMEM((tok, 3 * head), BF16),
             pltpu.VMEM((tok + erows, head), BF16),
             pltpu.VMEM((width, head), BF16),
-            pltpu.VMEM((dp, shard, head), BF16),
+            pltpu.VMEM((chunks, nc, shard, head), BF16),
+            pltpu.VMEM((chunks, shard, head), BF16),
+            pltpu.VMEM((chunks, shard, head), BF16),
+            pltpu.SemaphoreType.DMA((9,)),
             pltpu.SemaphoreType.DMA((2, dp)),
             pltpu.SemaphoreType.DMA((2, dp)),
             pltpu.SemaphoreType.DMA((chunks,)),
             pltpu.SemaphoreType.DMA((chunks,)),
-            pltpu.SemaphoreType.DMA((dp,)),
-            pltpu.SemaphoreType.DMA((dp,)),
+            pltpu.SemaphoreType.DMA((chunks, nc)),
+            pltpu.SemaphoreType.DMA((chunks, nc)),
+            pltpu.SemaphoreType.DMA((chunks,)),
+            pltpu.SemaphoreType.DMA((chunks,)),
         ],
         compiler_params=pltpu.CompilerParams(
             collective_id=0, has_side_effects=True, vmem_limit_bytes=48 * 1024 * 1024
@@ -413,14 +493,22 @@
         x_in[0],
         top_grad,
         norm_gain,
-        shards,
+        proj_in[0],
+        proj_out[0].T,
         key_cache[0],
         value_cache[0],
         prefix_len,
         early_out[0],
         early_dy[0],
     )
-    grad_x, key_grad, value_grad, wo_grad = outs
+    grad_x, key_grad, value_grad, wo_grad = pl.pallas_call(
+        results,
+        out_shape=[jax.ShapeDtypeStruct(out.shape, out.dtype) for out in outs],
+        in_specs=[vmem] * 4,
+        out_specs=[anywhere] * 4,
+        scratch_shapes=[pltpu.SemaphoreType.DMA((4,))],
+        name="results",
+    )(*outs)
     return grad_x[None], key_grad[None], value_grad[None], wo_grad.T[None]
 
 

time: 93.5 us -> 91.1 us (0.974)
  the two profiles are of different devices: /device:TPU:30 before, /device:TPU:0 now
where the time goes in v2:
time: 91.1 us; the launch traced here: 90.6 us
  Pallas kernels  77.7 us (85%)
  local copies, waits for them, and re-layouts  11.6 us (13%)
  between operations  1.32 us (1%)
    pallas_call x1, Pallas kernels, body(): pl.pallas_call(functools.partial(kernel, layers, (na, nb, nc)), out_shape...  75.1 us
    unnamed x26, local copies, waits for them, and re-layouts  11.6 us
    pallas_call x1, Pallas kernels, body(): pl.pallas_call(results, out_shape=[jax.ShapeDtypeStruct(out.shape, out.dt...  2.55 us

profile of v2, /device:TPU:0, one launch (start us, length us, event | category | flops | bytes accessed | tf_op | source)
XLA Modules:
  0.0 90.6 jit_solution(6980501498126782407)
XLA Ops:
  1.3 0.0 copy-start.4
  1.3 1.3 %copy-done.4 = bf16[1,128,5120]{2,1,0:T(8,128)(2,1)S(1)} copy-done((bf16[1,128,5120]{2,1,0:T(8,128)(2,1)S(1)}, bf16[1,128,5120]{2,1,0:T(8,128)(2,1)}, u32[]{:S(2)}) %copy-start.4) | copy-done | bytes 1310744
  2.6 0.0 copy-start.5
  2.6 1.3 %copy-done.5 = bf16[128,5120]{1,0:T(8,128)(2,1)S(1)} copy-done((bf16[128,5120]{1,0:T(8,128)(2,1)S(1)}, bf16[128,5120]{1,0:T(8,128)(2,1)}, u32[]{:S(2)}) %copy-start.5) | copy-done | bytes 1310744
  3.9 0.0 copy-start.6
  3.9 1.0 %copy-done.6 = bf16[1,32,5120]{2,1,0:T(8,128)(2,1)S(1)} copy-done((bf16[1,32,5120]{2,1,0:T(8,128)(2,1)S(1)}, bf16[1,32,5120]{2,1,0:T(8,128)(2,1)}, u32[]{:S(2)}) %copy-start.6) | copy-done | bytes 327704
  4.9 0.0 copy-start.7
  4.9 0.9 %copy-done.7 = bf16[1,320,384]{2,1,0:T(8,128)(2,1)S(1)} copy-done((bf16[1,320,384]{2,1,0:T(8,128)(2,1)S(1)}, bf16[1,320,384]{2,1,0:T(8,128)(2,1)}, u32[]{:S(2)}) %copy-start.7) | copy-done | bytes 245784
  5.8 0.0 copy-start.8
  5.8 0.9 copy-done.8
  6.7 0.0 copy-start.9
  6.7 0.9 copy-done.9
  7.6 0.0 copy-start.10
  7.6 0.9 copy-done.10
  8.5 0.0 copy-start.11
  8.5 0.7 copy-done.11
  9.2 0.0 copy-start.12
  9.2 0.7 copy-done.12
  9.9 75.1 %window_backward.1 = (bf16[128,5120]{1,0:T(8,128)(2,1)S(1)}, bf16[288,128]{1,0:T(8,128)(2,1)S(1)}, bf16[288,128]{1,0:T(8,128)(2,1)S(1)}, f32[320,128]{1,0:T(8,128)S(1)}) custom-call(bf16[128,5120]{1,0:T(8,128)(2,1)S(1)} %bitcast.15, bf16[128,5120]{1,0:T(8,128)(2,1)S(1)} %copy-done.5, bf16[1,5120]{1,0:T(2,128)(2,1)S(1)} %copy-done.11, ...), custom_call_target="tpu_custom_call" | custom-call | flops 2684354560 | bytes 5242880 | tf_op jit(solution)/shard_map/window_backward/pallas_call | solution.py:449
  85.0 0.0 copy-start
  85.0 1.1 %copy-done = bf16[128,5120]{1,0:T(8,128)(2,1)} copy-done((bf16[128,5120]{1,0:T(8,128)(2,1)}, bf16[128,5120]{1,0:T(8,128)(2,1)S(1)}, u32[]{:S(2)}) %copy-start) | copy-done | bytes 1310744
  86.1 0.0 copy-start.1
  86.1 0.7 copy-done.1
  86.8 0.0 copy-start.2
  86.8 0.6 copy-done.2
  87.4 0.0 copy-start.3
  87.4 0.6 copy-done.3
  88.0 2.6 %results.1 = (bf16[128,5120]{1,0:T(8,128)(2,1)}, bf16[288,128]{1,0:T(8,128)(2,1)}, bf16[288,128]{1,0:T(8,128)(2,1)}, f32[320,128]{1,0:T(8,128)}) custom-call(bf16[128,5120]{1,0:T(8,128)(2,1)} %copy-done, bf16[288,128]{1,0:T(8,128)(2,1)} %copy-done.2, bf16[288,128]{1,0:T(8,128)(2,1)} %copy-done.3, f32[320,128]{1,0:T(8,128)} %copy-done.1), custom_call_target="tpu_custom_call" | custom-call | tf_op jit(solution)/shard_map/results/pallas_call | solution.py:504
Async XLA Ops:
  1.3 1.3 %copy-start.4 = (bf16[1,128,5120]{2,1,0:T(8,128)(2,1)S(1)}, bf16[1,128,5120]{2,1,0:T(8,128)(2,1)}, u32[]{:S(2)}) copy-start(bf16[1,128,5120]{2,1,0:T(8,128)(2,1)} %param.10) | copy-start | bytes 3932164
  2.6 1.3 %copy-start.5 = (bf16[128,5120]{1,0:T(8,128)(2,1)S(1)}, bf16[128,5120]{1,0:T(8,128)(2,1)}, u32[]{:S(2)}) copy-start(bf16[128,5120]{1,0:T(8,128)(2,1)} %top_ref.1) | copy-start | bytes 3932164
  3.9 1.0 %copy-start.6 = (bf16[1,32,5120]{2,1,0:T(8,128)(2,1)S(1)}, bf16[1,32,5120]{2,1,0:T(8,128)(2,1)}, u32[]{:S(2)}) copy-start(bf16[1,32,5120]{2,1,0:T(8,128)(2,1)} %param.19) | copy-start | bytes 983044
  4.9 0.9 %copy-start.7 = (bf16[1,320,384]{2,1,0:T(8,128)(2,1)S(1)}, bf16[1,320,384]{2,1,0:T(8,128)(2,1)}, u32[]{:S(2)}) copy-start(bf16[1,320,384]{2,1,0:T(8,128)(2,1)} %param.13) | copy-start | bytes 737284
  5.8 0.9 copy-start.8
  6.7 0.9 copy-start.9
  7.6 0.9 copy-start.10
  8.5 0.7 copy-start.11
  9.2 0.7 copy-start.12
  85.0 1.1 %copy-start = (bf16[128,5120]{1,0:T(8,128)(2,1)}, bf16[128,5120]{1,0:T(8,128)(2,1)S(1)}, u32[]{:S(2)}) copy-start(bf16[128,5120]{1,0:T(8,128)(2,1)S(1)} %get-tuple-element.12.refs_0_) | copy-start | bytes 3932164
  86.1 0.7 copy-start.1
  86.8 0.6 copy-start.2
  87.4 0.6 copy-start.3

commit v3 on v2

--- a/solution.py
+++ b/solution.py
@@ -41,11 +41,16 @@
     plen_ref,
     eo_ref,
     edy_ref,
+    gx_hbm,
+    kg_hbm,
+    vg_hbm,
+    wo_hbm,
+    w,
+    inv_ref,
     gx_ref,
     kg_ref,
     vg_ref,
     wo_ref,
-    w,
     x_ref,
     normed,
     gin,
@@ -69,13 +74,16 @@
     m_recv,
     o_send,
     o_recv,
+    store,
+    store_gx,
+    gate,
 ):
     na, nb, nc = sizes
     dp = na * nb * nc
     sec = lax.axis_index("section")
     me = lax.axis_index("dp")
     top = layers - 1
-    tok, width = x_ref.shape
+    tok, width = x_hbm.shape
     head = kc_ref.shape[1]
     cache = kc_ref.shape[0]
     kpad = kall.shape[0]
@@ -171,43 +179,70 @@
         for m in range(1, nlast[h]):
             send(h, s, at(h, 0, 0, m))
 
-    for kz in range(1, na):
+    def open_gate(n):
+        @pl.when(sec > 0)
+        def _():
+            pl.semaphore_signal(gate.at[n], inc=1, device_id=(sec - 1, me), device_id_type=MESH)
+
+    def pass_gate(n):
+        @pl.when(sec < top)
+        def _():
+            pl.semaphore_wait(gate.at[n], 1)
+
+    def first_sends():
+        pass_gate(0)
+        for kz in range(1, na):
+            for h in range(2):
+                send(h, me, (kz, 0, 0))
+        pass_gate(1)
         for h in range(2):
-            send(h, me, (kz, 0, 0))
-    for h in range(2):
-        send_mid(h, me)
-    for h in range(2):
-        send_last(h, me)
-
-    if kpad > cache + tok:
-        kall[cache + tok :, :] = jnp.zeros((kpad - cache - tok, head), BF16)
-        vall[cache + tok :, :] = jnp.zeros((kpad - cache - tok, head), BF16)
-    qk_acc[...] = jnp.zeros_like(qk_acc)
-    v_acc[...] = jnp.zeros_like(v_acc)
-    go_acc[...] = jnp.zeros_like(go_acc)
-
-    for copy in loads[3:-1]:
-        copy.wait()
+            send_mid(h, me)
+        for h in range(2):
+            send_last(h, me)
+
+    def columns(c):
+        return pl.ds(pl.multiple_of(c * chunk, 128), chunk)
+
+    def prepare():
+        if kpad > cache + tok:
+            kall[cache + tok :, :] = jnp.zeros((kpad - cache - tok, head), BF16)
+            vall[cache + tok :, :] = jnp.zeros((kpad - cache - tok, head), BF16)
+        qk_acc[...] = jnp.zeros_like(qk_acc)
+        v_acc[...] = jnp.zeros_like(v_acc)
+        go_acc[...] = jnp.zeros_like(go_acc)
+
+        for copy in loads[3:-1]:
+            copy.wait()
+
+        @pl.when(sec == top)
+        def _():
+            loads[-1].wait()
+
+        def squares(c, total):
+            part = x_ref[:, columns(c)].astype(F32)
+            return total + jnp.sum(part * part, axis=1, keepdims=True)
+
+        total = lax.fori_loop(0, chunks, squares, jnp.zeros((tok, 1), F32))
+        inv_rms = lax.rsqrt(total / width + eps)
+        inv_ref[...] = jnp.broadcast_to(inv_rms, inv_ref.shape)
+
+        @pl.loop(0, chunks)
+        def _(c):
+            part = x_ref[:, columns(c)].astype(F32)
+            gain = gain_ref[:, columns(c)].astype(F32)
+            normed[:, columns(c)] = (part * inv_rms * gain).astype(BF16)
+
+    @pl.when(sec < top)
+    def _():
+        prepare()
+
+    first_sends()
 
     @pl.when(sec == top)
     def _():
-        loads[-1].wait()
-
-    def columns(c):
-        return pl.ds(pl.multiple_of(c * chunk, 128), chunk)
-
-    def squares(c, total):
-        part = x_ref[:, columns(c)].astype(F32)
-        return total + jnp.sum(part * part, axis=1, keepdims=True)
-
-    total = lax.fori_loop(0, chunks, squares, jnp.zeros((tok, 1), F32))
-    inv_rms = lax.rsqrt(total / width + eps)
-
-    @pl.loop(0, chunks)
-    def _(c):
-        part = x_ref[:, columns(c)].astype(F32)
-        gain = gain_ref[:, columns(c)].astype(F32)
-        normed[:, columns(c)] = (part * inv_rms * gain).astype(BF16)
+        prepare()
+
+    inv_rms = inv_ref[:, :1]
 
     def add_grad_out(c):
         go_acc[...] += dot(gin[:tok, columns(c)], w[1, columns(c), head:], 1, 0)
@@ -227,6 +262,35 @@
             def _():
                 add_grad_out(c)
 
+    def relay(c):
+        return pltpu.make_async_remote_copy(
+            src_ref=gx_ref.at[:, columns(c)],
+            dst_ref=gin.at[pl.ds(0, tok), columns(c)],
+            send_sem=g_send.at[c],
+            recv_sem=g_recv.at[c],
+            device_id=(jnp.maximum(sec - 1, 0), me),
+            device_id_type=MESH,
+        )
+
+    def relay_in(c):
+        return pltpu.make_async_remote_copy(
+            src_ref=gx_ref.at[:, columns(c)],
+            dst_ref=gin.at[pl.ds(0, tok), columns(c)],
+            send_sem=g_send.at[c],
+            recv_sem=g_recv.at[c],
+            device_id=(jnp.minimum(sec + 1, top), me),
+            device_id_type=MESH,
+        )
+
+    def late_grad_out(phases):
+        @pl.when(sec < top)
+        def _():
+            for kz in phases:
+                for ky in range(nb):
+                    c = other(mz, kz, na) * nb + other(my, ky, nb)
+                    relay_in(c).wait_recv()
+                    add_grad_out(c)
+
     for kz in range(na):
         if kz > 0:
             for h in range(2):
@@ -234,6 +298,8 @@
                 arrive(h, s)
                 send_mid(h, s)
                 send_last(h, s)
+        if kz == na - 1:
+            open_gate(0)
         for h in range(2):
             for m in range(1, nmid[h]):
                 s = sid(*at(h, kz, m, 0))
@@ -241,7 +307,10 @@
                 send_last(h, s)
         if kz > 0:
             use(kz - 1)
+    open_gate(1)
+    late_grad_out(range(na - 1))
     use(na - 1)
+    late_grad_out([na - 1])
 
     query = qk_acc[:, :head].astype(BF16)
     kall[cache : cache + tok, :] = qk_acc[:, head:].astype(BF16)
@@ -257,26 +326,6 @@
     prob_low = prob.astype(BF16)
     atte[:tok, :] = dot(prob_low, vall[...], 1, 0).astype(BF16)
 
-    def relay(c):
-        return pltpu.make_async_remote_copy(
-            src_ref=gx_ref.at[:, columns(c)],
-            dst_ref=gin.at[pl.ds(0, tok), columns(c)],
-            send_sem=g_send.at[c],
-            recv_sem=g_recv.at[c],
-            device_id=(jnp.maximum(sec - 1, 0), me),
-            device_id_type=MESH,
-        )
-
-    def relay_in(c):
-        return pltpu.make_async_remote_copy(
-            src_ref=gx_ref.at[:, columns(c)],
-            dst_ref=gin.at[pl.ds(0, tok), columns(c)],
-            send_sem=g_send.at[c],
-            recv_sem=g_recv.at[c],
-            device_id=(jnp.minimum(sec + 1, top), me),
-            device_id_type=MESH,
-        )
-
     group = me // nc
 
     def order(i):
@@ -328,11 +377,6 @@
     @pl.loop(0, chunks)
     def _(i):
         c = order(i)
-
-        @pl.when(sec < top)
-        def _():
-            relay_in(c).wait_recv()
-            add_grad_out(c)
 
         wo_chunk(c)
 
@@ -349,6 +393,20 @@
     grad_values = dot(prob_low, grad_out, 0, 0)
     kg_ref[...] = grad_keys[:cache].astype(BF16)
     vg_ref[...] = grad_values[:cache].astype(BF16)
+    stores = [
+        pltpu.make_async_copy(source, target, store.at[n])
+        for n, (source, target) in enumerate(
+            [(kg_ref, kg_hbm), (vg_ref, vg_hbm), (wo_ref, wo_hbm)]
+        )
+    ]
+    stores[0].start()
+    stores[1].start()
+
+    def store_part(c):
+        return pltpu.make_async_copy(
+            gx_ref.at[:, columns(c)], gx_hbm.at[:, columns(c)], store_gx.at[c]
+        )
+
     gproj[:, :head] = grad_query.astype(BF16)
     gproj[:, head : 2 * head] = grad_keys[cache : cache + tok].astype(BF16)
     gproj[:, 2 * head :] = grad_values[cache : cache + tok].astype(BF16)
@@ -373,6 +431,8 @@
         branch = inv_rms * scaled - x_ref[:, columns(c)].astype(F32) * pull
         gx_ref[:, columns(c)] = (gin[:tok, columns(c)].astype(F32) + branch).astype(BF16)
 
+        store_part(c).start()
+
         @pl.when(sec > 0)
         def _():
             relay(c).start()
@@ -403,6 +463,14 @@
         return part + wo_in[source].astype(F32)
 
     wo_ref[...] = lax.fori_loop(0, chunks - 1, gathered, wo_sum[group].astype(F32))
+    stores[2].start()
+
+    @pl.loop(0, chunks)
+    def _(c):
+        store_part(c).wait()
+
+    for copy in stores:
+        copy.wait()
 
 
 def results(*refs):
@@ -455,9 +523,14 @@
             jax.ShapeDtypeStruct((shard, head), F32),
         ),
         in_specs=[anywhere] * 2 + [vmem] + [anywhere] * 4 + [smem] + [anywhere] * 2,
-        out_specs=(vmem,) * 4,
+        out_specs=(anywhere,) * 4,
         scratch_shapes=[
             pltpu.VMEM((2, width, 2 * head), BF16),
+            pltpu.VMEM((tok, 128), F32),
+            pltpu.VMEM((tok, width), BF16),
+            pltpu.VMEM((cache, head), BF16),
+            pltpu.VMEM((cache, head), BF16),
+            pltpu.VMEM((shard, head), F32),
             pltpu.VMEM((tok, width), BF16),
             pltpu.VMEM((tok, width), BF16),
             pltpu.VMEM((tok + erows, width), BF16),
@@ -481,9 +554,12 @@
             pltpu.SemaphoreType.DMA((chunks, nc)),
             pltpu.SemaphoreType.DMA((chunks,)),
             pltpu.SemaphoreType.DMA((chunks,)),
+            pltpu.SemaphoreType.DMA((3,)),
+            pltpu.SemaphoreType.DMA((chunks,)),
+            pltpu.SemaphoreType.REGULAR((2,)),
         ],
         compiler_params=pltpu.CompilerParams(
-            collective_id=0, has_side_effects=True, vmem_limit_bytes=48 * 1024 * 1024
+            collective_id=0, has_side_effects=True, vmem_limit_bytes=62 * 1024 * 1024
         ),
         cost_estimate=pl.CostEstimate(
             flops=8 * tok * width * head * 4, bytes_accessed=8 * tok * width, transcendentals=0
@@ -504,9 +580,10 @@
     grad_x, key_grad, value_grad, wo_grad = pl.pallas_call(
         results,
         out_shape=[jax.ShapeDtypeStruct(out.shape, out.dtype) for out in outs],
-        in_specs=[vmem] * 4,
+        in_specs=[anywhere] * 4,
         out_specs=[anywhere] * 4,
         scratch_shapes=[pltpu.SemaphoreType.DMA((4,))],
+        compiler_params=pltpu.CompilerParams(vmem_limit_bytes=62 * 1024 * 1024),
         name="results",
     )(*outs)
     return grad_x[None], key_grad[None], value_grad[None], wo_grad.T[None]

time: 91.1 us -> 138 us (1.51)
  Pallas kernels: 77.7 us -> 137 us
  local copies, waits for them, and re-layouts: 11.6 us -> 0 us
    pallas_call x1, Pallas kernels: 2.55 us -> 50.3 us  [body(): pl.pallas_call(results, out_shape=[jax.ShapeDtypeStruct(out.shape, out.dt...]
    unnamed x26 -> x0, local copies, waits for them, and re-layouts: 11.6 us -> none
    pallas_call x1, Pallas kernels: 75.1 us -> 86.4 us  [body(): pl.pallas_call(functools.partial(kernel, layers, (na, nb, nc)), out_shape...]
where the time goes in v3:
time: 138 us
  Pallas kernels  137 us (99%)
    pallas_call x1, Pallas kernels, body(): pl.pallas_call(functools.partial(kernel, layers, (na, nb, nc)), out_shape...  86.4 us
    pallas_call x1, Pallas kernels, body(): pl.pallas_call(results, out_shape=[jax.ShapeDtypeStruct(out.shape, out.dt...  50.3 us

profile of v3, /device:TPU:0, one launch (start us, length us, event | category | flops | bytes accessed | tf_op | source)
XLA Modules:
  0.0 138.0 jit_solution(10266965588908218030)
XLA Ops:
  1.3 86.4 %window_backward.1 = (bf16[128,5120]{1,0:T(8,128)(2,1)}, bf16[288,128]{1,0:T(8,128)(2,1)}, bf16[288,128]{1,0:T(8,128)(2,1)}, f32[320,128]{1,0:T(8,128)}) custom-call(bf16[128,5120]{1,0:T(8,128)(2,1)} %bitcast.15, bf16[128,5120]{1,0:T(8,128)(2,1)} %top_ref.1, bf16[1,5120]{1,0:T(2,128)(2,1)} %gain_ref.1, bf16[320,384]{1,0:T(8,128)(2,1)} %bitcast.18, ...), custom_call_target="tpu_custom_call" | custom-call | flops 2684354560 | bytes 5242880 | tf_op jit(solution)/shard_map/window_backward/pallas_call | solution.py:517
  87.7 50.3 %results.1 = (bf16[128,5120]{1,0:T(8,128)(2,1)}, bf16[288,128]{1,0:T(8,128)(2,1)}, bf16[288,128]{1,0:T(8,128)(2,1)}, f32[320,128]{1,0:T(8,128)}) custom-call(bf16[128,5120]{1,0:T(8,128)(2,1)} %get-tuple-element.12.refs_0_, bf16[288,128]{1,0:T(8,128)(2,1)} %get-tuple-element.13.refs_1_, bf16[288,128]{1,0:T(8,128)(2,1)} %get-tuple-element.14.refs_2_, ...), custom_call_target="tpu_custom_call" | custom-call | tf_op jit(solution)/shard_map/results/pallas_call | solution.py:580

commit v4 on v3

--- a/solution.py
+++ b/solution.py
@@ -76,7 +76,6 @@
     o_recv,
     store,
     store_gx,
-    gate,
 ):
     na, nb, nc = sizes
     dp = na * nb * nc
@@ -179,22 +178,10 @@
         for m in range(1, nlast[h]):
             send(h, s, at(h, 0, 0, m))
 
-    def open_gate(n):
-        @pl.when(sec > 0)
-        def _():
-            pl.semaphore_signal(gate.at[n], inc=1, device_id=(sec - 1, me), device_id_type=MESH)
-
-    def pass_gate(n):
-        @pl.when(sec < top)
-        def _():
-            pl.semaphore_wait(gate.at[n], 1)
-
     def first_sends():
-        pass_gate(0)
         for kz in range(1, na):
             for h in range(2):
                 send(h, me, (kz, 0, 0))
-        pass_gate(1)
         for h in range(2):
             send_mid(h, me)
         for h in range(2):
@@ -232,15 +219,8 @@
             gain = gain_ref[:, columns(c)].astype(F32)
             normed[:, columns(c)] = (part * inv_rms * gain).astype(BF16)
 
-    @pl.when(sec < top)
-    def _():
-        prepare()
-
     first_sends()
-
-    @pl.when(sec == top)
-    def _():
-        prepare()
+    prepare()
 
     inv_rms = inv_ref[:, :1]
 
@@ -282,15 +262,6 @@
             device_id_type=MESH,
         )
 
-    def late_grad_out(phases):
-        @pl.when(sec < top)
-        def _():
-            for kz in phases:
-                for ky in range(nb):
-                    c = other(mz, kz, na) * nb + other(my, ky, nb)
-                    relay_in(c).wait_recv()
-                    add_grad_out(c)
-
     for kz in range(na):
         if kz > 0:
             for h in range(2):
@@ -298,8 +269,6 @@
                 arrive(h, s)
                 send_mid(h, s)
                 send_last(h, s)
-        if kz == na - 1:
-            open_gate(0)
         for h in range(2):
             for m in range(1, nmid[h]):
                 s = sid(*at(h, kz, m, 0))
@@ -307,10 +276,7 @@
                 send_last(h, s)
         if kz > 0:
             use(kz - 1)
-    open_gate(1)
-    late_grad_out(range(na - 1))
     use(na - 1)
-    late_grad_out([na - 1])
 
     query = qk_acc[:, :head].astype(BF16)
     kall[cache : cache + tok, :] = qk_acc[:, head:].astype(BF16)
@@ -377,6 +343,12 @@
     @pl.loop(0, chunks)
     def _(i):
         c = order(i)
+
+
+        @pl.when(sec < top)
+        def _():
+            relay_in(c).wait_recv()
+            add_grad_out(c)
 
         wo_chunk(c)
 
@@ -556,7 +528,6 @@
             pltpu.SemaphoreType.DMA((chunks,)),
             pltpu.SemaphoreType.DMA((3,)),
             pltpu.SemaphoreType.DMA((chunks,)),
-            pltpu.SemaphoreType.REGULAR((2,)),
         ],
         compiler_params=pltpu.CompilerParams(
             collective_id=0, has_side_effects=True, vmem_limit_bytes=62 * 1024 * 1024
@@ -580,7 +551,7 @@
     grad_x, key_grad, value_grad, wo_grad = pl.pallas_call(
         results,
         out_shape=[jax.ShapeDtypeStruct(out.shape, out.dtype) for out in outs],
-        in_specs=[anywhere] * 4,
+        in_specs=[vmem] * 4,
         out_specs=[anywhere] * 4,
         scratch_shapes=[pltpu.SemaphoreType.DMA((4,))],
         compiler_params=pltpu.CompilerParams(vmem_limit_bytes=62 * 1024 * 1024),

time: 138 us -> 80.7 us (0.58)
  Pallas kernels: 137 us -> 79.2 us
    pallas_call x1, Pallas kernels: 50.3 us -> 2.56 us  [body(): pl.pallas_call(results, out_shape=[jax.ShapeDtypeStruct(out.shape, out.dt...]
    pallas_call x1, Pallas kernels: 86.4 us -> 76.6 us  [body(): pl.pallas_call(functools.partial(kernel, layers, (na, nb, nc)), out_shape...]
where the time goes in v4:
time: 80.7 us; the launch traced here: 80.5 us
  Pallas kernels  79.2 us (98%)
  between operations  1.29 us (2%)
    pallas_call x1, Pallas kernels, body(): pl.pallas_call(functools.partial(kernel, layers, (na, nb, nc)), out_shape...  76.6 us
    pallas_call x1, Pallas kernels, body(): pl.pallas_call(results, out_shape=[jax.ShapeDtypeStruct(out.shape, out.dt...  2.56 us

profile of v4, /device:TPU:0, one launch (start us, length us, event | category | flops | bytes accessed | tf_op | source)
XLA Modules:
  0.0 80.5 jit_solution(9588632310520184124)
XLA Ops:
  1.3 76.6 %window_backward.1 = (bf16[128,5120]{1,0:T(8,128)(2,1)}, bf16[288,128]{1,0:T(8,128)(2,1)}, bf16[288,128]{1,0:T(8,128)(2,1)}, f32[320,128]{1,0:T(8,128)}) custom-call(bf16[128,5120]{1,0:T(8,128)(2,1)} %bitcast.15, bf16[128,5120]{1,0:T(8,128)(2,1)} %top_ref.1, bf16[1,5120]{1,0:T(2,128)(2,1)} %gain_ref.1, bf16[320,384]{1,0:T(8,128)(2,1)} %bitcast.18, ...), custom_call_target="tpu_custom_call" | custom-call | flops 2684354560 | bytes 5242880 | tf_op jit(solution)/shard_map/window_backward/pallas_call | solution.py:489
  77.9 2.6 %results.1 = (bf16[128,5120]{1,0:T(8,128)(2,1)}, bf16[288,128]{1,0:T(8,128)(2,1)}, bf16[288,128]{1,0:T(8,128)(2,1)}, f32[320,128]{1,0:T(8,128)}) custom-call(bf16[128,5120]{1,0:T(8,128)(2,1)} %get-tuple-element.12.refs_0_, bf16[288,128]{1,0:T(8,128)(2,1)} %get-tuple-element.13.refs_1_, bf16[288,128]{1,0:T(8,128)(2,1)} %get-tuple-element.14.refs_2_, ...), custom_call_target="tpu_custom_call" | custom-call | tf_op jit(solution)/shard_map/results/pallas_call | solution.py:551
